TPU v7x, 32 devices: a whole 2x2x4 slice. The times are simulated.
32 devices in a mesh: group: 4 (over z), shard: 8 (over y, x, core).
Axes of the slice: x: 2, y: 2, z: 4, core: 2. Of those that a mesh axis runs over, the one named last changes fastest.
Arguments:
- hot_row: int32 [256, 39], P(('group', 'shard')), may hold values from 0 to 2047
- cold_row: int32 [256, 39], P(('group', 'shard')), may hold values from 0 to 4095
- cold_owner: int32 [256, 39], P(('group', 'shard')), may hold values from 0 to 7, as said below
- is_cold: int32 [256, 39], P(('group', 'shard')), may hold values from 0 to 1
- grad_logit: float32 [256], P(('group', 'shard')), may hold values from -12 to 12
- hot_table: bfloat16 [2048, 128], replicated, may hold values from -6 to 6
- cold_table: bfloat16 [32768, 128], P('shard'), may hold values from -6 to 6
- first_weight: bfloat16 [100, 1521], replicated, may hold values from -0.15625 to 0.15625
- second_weight: bfloat16 [100, 3900], replicated, may hold values from -0.09375 to 0.09375
- third_weight: bfloat16 [100, 3900], replicated, may hold values from -0.09375 to 0.09375
- out_weight: float32 [3, 100], replicated, may hold values from -0.375 to 0.375
Outputs:
- hot_grad: bfloat16 [2048, 128], replicated
- cold_grad: bfloat16 [32768, 128], P('shard')
- logits: float32 [256], P(('group', 'shard'))
Inputs may be any that keep to these rules, and one draw needn't show every extreme that they name: `cold_owner`: among the 312 lookups of one device, at most 39 with is_cold 1 name the same owner; for each index of group, one owner receives exactly 39 such lookups from every device of that group index.
All inputs are finite; a program needn't handle non-finite values.
Results may differ from a plain program's by a relative error of at most 0.014.
Values may be sent and summed in bfloat16 or wider, within the bound.
A program may use at most 64 MiB of HBM per device.

v0:
```python
import jax
import jax.numpy as jnp
from jax import lax
from jax.sharding import PartitionSpec as P


def sample_pass(embedded, grad_logit, layer_weights, out_weight):
    batch_rows, fields, breadth = embedded.shape
    base_wide = embedded.astype(jnp.float32)
    previous = embedded
    layer_inputs = []
    logit_sum = jnp.zeros((batch_rows,), jnp.float32)
    for section_index in range(len(layer_weights)):
        weight = layer_weights[section_index]
        below_maps = previous.shape[1]
        outer_rows = (
            previous.astype(jnp.float32)[:, :, None, :] * base_wide[:, None, :, :]
        ).astype(jnp.bfloat16)
        outer_rows = outer_rows.reshape(batch_rows, below_maps * fields, breadth)
        current = jnp.einsum(
            "hk,bke->bhe", weight, outer_rows, preferred_element_type=jnp.float32
        ).astype(jnp.bfloat16)
        pooled = jnp.sum(current.astype(jnp.float32), axis=2)
        logit_sum = logit_sum + jnp.sum(pooled * out_weight[section_index][None, :], axis=1)
        layer_inputs.append(previous)
        previous = current
    grad_embedded = jnp.zeros((batch_rows, fields, breadth), jnp.float32)
    carried = jnp.zeros((batch_rows, out_weight.shape[1], breadth), jnp.float32)
    for section_index in reversed(range(len(layer_weights))):
        weight = layer_weights[section_index]
        lower_state = layer_inputs[section_index]
        below_maps = lower_state.shape[1]
        grad_state = carried + grad_logit[:, None, None] * out_weight[section_index][None, :, None]
        grad_low = grad_state.astype(jnp.bfloat16)
        grad_outer = jnp.einsum("hk,bhe->bke", weight, grad_low, preferred_element_type=jnp.float32)
        grad_outer = grad_outer.reshape(batch_rows, below_maps, fields, breadth)
        grad_embedded = grad_embedded + jnp.sum(
            grad_outer * lower_state.astype(jnp.float32)[:, :, None, :], axis=1
        )
        carried = jnp.sum(grad_outer * base_wide[:, None, :, :], axis=2)
    grad_embedded = grad_embedded + carried
    return (logit_sum, grad_embedded)


def local(
    hot_row,
    cold_row,
    cold_owner,
    is_cold,
    grad_logit,
    hot_table,
    cold_table,
    first_weight,
    second_weight,
    third_weight,
    out_weight,
):
    samples, fields = hot_row.shape
    breadth = hot_table.shape[1]
    owners = lax.axis_size("shard")
    lookups = samples * fields
    capacity = lookups // owners
    owner_flat = cold_owner.reshape(lookups)
    cold_flag = is_cold.reshape(lookups) == 1
    wanted = jnp.logical_and(
        owner_flat[:, None] == jnp.arange(owners, dtype=jnp.int32)[None, :], cold_flag[:, None]
    ).astype(jnp.int32)
    earlier = jnp.cumsum(wanted, axis=0) - wanted
    position = jnp.sum(earlier * wanted, axis=1)
    target = jnp.where(cold_flag, owner_flat * capacity + position, owners * capacity)
    asked_rows = jnp.where(cold_flag, cold_row.reshape(lookups), -1)
    request = jnp.full((owners * capacity + 1,), -1, jnp.int32).at[target].set(asked_rows)
    request = request[: owners * capacity].reshape(owners, capacity)
    requested = lax.all_to_all(request, "shard", split_axis=0, concat_axis=0, tiled=True)
    present = requested >= 0
    table_rows = jnp.take(cold_table, jnp.maximum(requested, 0), axis=0)
    table_rows = jnp.where(present[:, :, None], table_rows, jnp.zeros_like(table_rows))
    returned = lax.all_to_all(table_rows, "shard", split_axis=0, concat_axis=0, tiled=True)
    fetched_flat = jnp.concatenate(
        [returned.reshape(owners * capacity, breadth), jnp.zeros((1, breadth), jnp.bfloat16)],
        axis=0,
    )
    cold_values = jnp.take(fetched_flat, target, axis=0)
    hot_values = jnp.take(hot_table, hot_row.reshape(lookups), axis=0)
    embedded = jnp.where(cold_flag[:, None], cold_values, hot_values).reshape(
        samples, fields, breadth
    )
    layer_weights = (first_weight, second_weight, third_weight)

    def one_sample(sample_pair):
        logit_one, grad_one = sample_pass(
            sample_pair[0][None], sample_pair[1][None], layer_weights, out_weight
        )
        return (logit_one[0], grad_one[0])

    logits, gradients = lax.map(one_sample, (embedded, grad_logit))
    gradients = gradients.reshape(lookups, breadth)
    cold_terms = jnp.where(cold_flag[:, None], gradients, 0.0)
    hot_terms = jnp.where(cold_flag[:, None], 0.0, gradients)
    outgoing = jnp.zeros((owners * capacity + 1, breadth), jnp.float32).at[target].add(cold_terms)
    outgoing = outgoing[: owners * capacity].reshape(owners, capacity, breadth)
    incoming = lax.all_to_all(
        outgoing.astype(jnp.bfloat16), "shard", split_axis=0, concat_axis=0, tiled=True
    ).astype(outgoing.dtype)
    shard_rows = cold_table.shape[0]
    safe_ids = jnp.maximum(requested, 0)
    cold_local = jax.ops.segment_sum(
        incoming.reshape(-1, breadth), safe_ids.reshape(-1), num_segments=shard_rows
    )
    cold_total = lax.psum(cold_local.astype(jnp.bfloat16), "group")
    hot_local = jax.ops.segment_sum(
        hot_terms, hot_row.reshape(lookups), num_segments=hot_table.shape[0]
    )
    hot_grad = lax.psum(hot_local, ("group", "shard")).astype(jnp.bfloat16)
    return (hot_grad, cold_total, logits)


def solution(mesh):
    return jax.shard_map(
        local,
        mesh=mesh,
        in_specs=(
            P(("group", "shard"), None),
            P(("group", "shard"), None),
            P(("group", "shard"), None),
            P(("group", "shard"), None),
            P(("group", "shard")),
            P(),
            P("shard", None),
            P(),
            P(),
            P(),
            P(),
        ),
        out_specs=(P(), P("shard", None), P(("group", "shard"))),
        check_vma=False,
    )
```

profile of v0, /device:TPU:0, one launch (start us, length us, event | category | flops | bytes accessed | tf_op | source)
XLA Modules:
  0.0 282.2 jit_solution(10971095908079539515)
XLA Ops:
  11.8 2.9 %scatter_custom_fusion = s32[313]{0:T(512)S(1)} fusion(s32[312]{0:T(512)S(1)} %fusion.26, s32[312]{0:T(512)S(1)} %broadcast_select_fusion, s32[]{:T(128)} %constant.56.clone.1), kind=kCustom, calls=%fused_computation.84 | custom fusion | bytes 1256 | tf_op jit(solution)/shard_map/scatter | solution.py:72
  15.4 5.2 %all-to-all-start = ((s32[8,1,39]{2,1,0:T(1,128)}), s32[8,1,39]{2,1,0:T(1,128)S(1)}, u32[]{:S(2)}, u32[]{:S(2)}) async-start(s32[8,1,39]{2,1,0:T(1,128)} %all_to_all.12), calls=%async_computation | async-start | bytes 8192 | tf_op jit(solution)/shard_map/all_to_all | solution.py:74
  22.2 2.2 gather_fusion.2
  27.5 3.6 %all-to-all-start.1 = ((bf16[8,39,128]{2,1,0:T(8,128)(2,1)}), bf16[8,39,128]{2,1,0:T(8,128)(2,1)S(1)}, u32[]{:S(2)}, u32[]{:S(2)}) async-start(bf16[8,39,128]{2,1,0:T(8,128)(2,1)} %select_select_fusion.1), calls=%async_computation.1 | async-start | bytes 163840 | tf_op jit(solution)/shard_map/all_to_all | solution.py:78
  31.1 5.0 %all-to-all-done.1 = bf16[8,39,128]{2,1,0:T(8,128)(2,1)S(1)} async-done(((bf16[8,39,128]{2,1,0:T(8,128)(2,1)}), bf16[8,39,128]{2,1,0:T(8,128)(2,1)S(1)}, u32[]{:S(2)}, u32[]{:S(2)}) %all-to-all-start.1) | async-done | bytes 79904 | tf_op jit(solution)/shard_map/all_to_all | solution.py:78
  38.5 165.5 %while.12 = (s32[]{:T(128)}, f32[8]{0:T(128)}, f32[8,39,128]{2,1,0:T(8,128)}, bf16[8,39,128]{2,1,0:T(8,128)(2,1)}, bf16[100,1521]{1,0:T(8,128)(2,1)S(1)}, /*inde...) while((s32[]{:T(128)}, f32[8]{0:T(128)}, ...), condition=%wide.region_17.18_spmd, body=%wide.region_4.17_spmd.sunk | while | flops 484535232 | bytes 39531044 | solution.py:96
  40.3 1.6 fusion.65
  42.4 1.7 fusion.66
  46.8 1.8 convolution_bitcast_fusion.6
  51.4 1.8 convolution_bitcast_fusion.7
  61.0 1.6 fusion.65
  63.1 1.7 fusion.66
  67.5 1.8 convolution_bitcast_fusion.6
  72.1 1.8 convolution_bitcast_fusion.7
  73.9 1.6 reshape.546
  81.7 1.6 fusion.65
  83.8 1.7 fusion.66
  88.2 1.8 convolution_bitcast_fusion.6
  90.0 1.6 reshape.545
  92.8 1.8 convolution_bitcast_fusion.7
  94.6 1.6 reshape.546
  102.3 1.6 fusion.65
  104.5 1.7 fusion.66
  108.9 1.8 convolution_bitcast_fusion.6
  110.7 1.6 reshape.545
  113.4 1.8 convolution_bitcast_fusion.7
  123.0 1.6 fusion.65
  125.2 1.7 fusion.66
  129.5 1.8 convolution_bitcast_fusion.6
  134.1 1.8 convolution_bitcast_fusion.7
  143.7 1.6 fusion.65
  145.9 1.7 fusion.66
  150.2 1.8 convolution_bitcast_fusion.6
  154.8 1.8 convolution_bitcast_fusion.7
  164.4 1.6 fusion.65
  166.5 1.7 fusion.66
  170.9 1.8 convolution_bitcast_fusion.6
  175.5 1.8 convolution_bitcast_fusion.7
  185.1 1.6 fusion.65
  187.2 1.7 fusion.66
  191.6 1.8 convolution_bitcast_fusion.6
  196.2 1.8 convolution_bitcast_fusion.7
  204.9 1.9 scatter_custom_fusion.2
  206.9 7.5 %all_to_all.19 = bf16[8,39,128]{2,1,0:T(8,128)(2,1)S(1)} all-to-all(bf16[8,39,128]{2,1,0:T(8,128)(2,1)S(1)} %convert_element_type.112), channel_id=1, replica_groups=mesh['group'=4,'shard'=8] {'shard'}, dimensions={0} | all-to-all | bytes 159744 | tf_op jit(solution)/shard_map/all_to_all | solution.py:102
  214.4 2.5 scatter_custom_fusion.3
  218.1 2.0 scatter_custom_fusion.1
  220.1 53.0 %all-reduce.6 = bf16[2048,128]{1,0:T(8,128)(2,1)} all-reduce(f32[2048,128]{1,0:T(8,128)S(1)} %scatter_custom_fusion.1), channel_id=1, replica_groups=mesh['group'=4,'shard'=8] {'group','shard'}, use_global_device_ids=true, to_apply=%region_19.20 | all-reduce | flops 262144 | bytes 1572864 | tf_op jit(solution)/shard_map/psum | solution.py:114
  273.1 2.3 copy.32
  (292 shorter events, 102.0 us)
Async XLA Ops:
  7.2 18.1 %copy-start = (bf16[4096,128]{1,0:T(8,128)(2,1)S(1)}, bf16[4096,128]{1,0:T(8,128)(2,1)}, u32[]{:S(2)}) copy-start(bf16[4096,128]{1,0:T(8,128)(2,1)} %param.19) | copy-start | bytes 3145732
  7.2 31.3 %copy-start.3 = (bf16[100,1521]{1,0:T(8,128)(2,1)S(1)}, bf16[100,1521]{1,0:T(8,128)(2,1)}, u32[]{:S(2)}) copy-start(bf16[100,1521]{1,0:T(8,128)(2,1)} %param.20) | copy-start | bytes 912604
  7.2 31.3 %copy-start.6 = (f32[3,100]{1,0:T(4,128)S(1)}, f32[3,100]{1,0:T(4,128)}, u32[]{:S(2)}) copy-start(f32[3,100]{1,0:T(4,128)} %param.23) | copy-start | bytes 3604
  8.1 30.4 %copy-start.7 = (pred[312]{0:T(512)(128)(4,1)}, pred[312]{0:T(512)(128)(4,1)S(1)}, u32[]{:S(2)}) copy-start(pred[312]{0:T(512)(128)(4,1)S(1)} %eq.48) | copy-start | bytes 940
  11.8 26.7 %copy-start.9 = (s32[312]{0:T(512)}, s32[312]{0:T(512)S(1)}, u32[]{:S(2)}) copy-start(s32[312]{0:T(512)S(1)} %fusion.26) | copy-start | bytes 3748
  15.4 9.8 %all-to-all-start = ((s32[8,1,39]{2,1,0:T(1,128)}), s32[8,1,39]{2,1,0:T(1,128)S(1)}, u32[]{:S(2)}, u32[]{:S(2)}) async-start(s32[8,1,39]{2,1,0:T(1,128)} %all_to_all.12), calls=%async_computation | async-start | bytes 8192 | tf_op jit(solution)/shard_map/all_to_all | solution.py:74
  25.2 5.8 %copy-start.10 = (s32[312]{0:T(512)}, s32[312]{0:T(512)S(1)}, u32[]{:S(2)}) copy-start(s32[312]{0:T(512)S(1)} %reshape.473) | copy-start | bytes 3748
  27.5 8.7 %all-to-all-start.1 = ((bf16[8,39,128]{2,1,0:T(8,128)(2,1)}), bf16[8,39,128]{2,1,0:T(8,128)(2,1)S(1)}, u32[]{:S(2)}, u32[]{:S(2)}) async-start(bf16[8,39,128]{2,1,0:T(8,128)(2,1)} %select_select_fusion.1), calls=%async_computation.1 | async-start | bytes 163840 | tf_op jit(solution)/shard_map/all_to_all | solution.py:78
  31.1 242.0 %all-reduce.5.cloned.1.call-start = ((), (), s32[]{:S(2)}) async-start(), calls=%async_computation.3 | async-start | bytes 2097152 | tf_op jit(solution)/shard_map/psum | solution.py:110
  42.4 4.4 %copy-start.2 = (bf16[100,3900]{1,0:T(8,128)(2,1)S(1)}, bf16[100,3900]{1,0:T(8,128)(2,1)}, u32[]{:S(2)}) copy-start(bf16[100,3900]{1,0:T(8,128)(2,1)} %get-tuple-element.208) | copy-start | bytes 2340004 | tf_op jit(solution)/shard_map/while
  50.2 1.1 copy-start.1
  55.4 0.7 copy-start.4
  55.5 3.1 %copy-start.11 = (f32[8]{0:T(128)S(1)}, f32[8]{0:T(128)}, u32[]{:S(2)}) copy-start(f32[8]{0:T(128)} %get-tuple-element.192) | copy-start | bytes 100 | tf_op jit(solution)/shard_map/while
  58.7 0.5 copy-start.12
  63.1 4.4 %copy-start.2 = (bf16[100,3900]{1,0:T(8,128)(2,1)S(1)}, bf16[100,3900]{1,0:T(8,128)(2,1)}, u32[]{:S(2)}) copy-start(bf16[100,3900]{1,0:T(8,128)(2,1)} %get-tuple-element.208) | copy-start | bytes 2340004 | tf_op jit(solution)/shard_map/while
  70.9 1.1 copy-start.1
  76.1 0.7 copy-start.4
  76.1 3.1 %copy-start.11 = (f32[8]{0:T(128)S(1)}, f32[8]{0:T(128)}, u32[]{:S(2)}) copy-start(f32[8]{0:T(128)} %get-tuple-element.192) | copy-start | bytes 100 | tf_op jit(solution)/shard_map/while
  79.4 0.5 copy-start.12
  83.8 4.4 %copy-start.2 = (bf16[100,3900]{1,0:T(8,128)(2,1)S(1)}, bf16[100,3900]{1,0:T(8,128)(2,1)}, u32[]{:S(2)}) copy-start(bf16[100,3900]{1,0:T(8,128)(2,1)} %get-tuple-element.208) | copy-start | bytes 2340004 | tf_op jit(solution)/shard_map/while
  91.6 1.1 copy-start.1
  96.8 0.7 copy-start.4
  96.8 3.1 %copy-start.11 = (f32[8]{0:T(128)S(1)}, f32[8]{0:T(128)}, u32[]{:S(2)}) copy-start(f32[8]{0:T(128)} %get-tuple-element.192) | copy-start | bytes 100 | tf_op jit(solution)/shard_map/while
  100.1 0.5 copy-start.12
  104.5 4.4 %copy-start.2 = (bf16[100,3900]{1,0:T(8,128)(2,1)S(1)}, bf16[100,3900]{1,0:T(8,128)(2,1)}, u32[]{:S(2)}) copy-start(bf16[100,3900]{1,0:T(8,128)(2,1)} %get-tuple-element.208) | copy-start | bytes 2340004 | tf_op jit(solution)/shard_map/while
  112.3 1.1 copy-start.1
  117.5 0.7 copy-start.4
  117.5 3.1 %copy-start.11 = (f32[8]{0:T(128)S(1)}, f32[8]{0:T(128)}, u32[]{:S(2)}) copy-start(f32[8]{0:T(128)} %get-tuple-element.192) | copy-start | bytes 100 | tf_op jit(solution)/shard_map/while
  125.2 4.4 %copy-start.2 = (bf16[100,3900]{1,0:T(8,128)(2,1)S(1)}, bf16[100,3900]{1,0:T(8,128)(2,1)}, u32[]{:S(2)}) copy-start(bf16[100,3900]{1,0:T(8,128)(2,1)} %get-tuple-element.208) | copy-start | bytes 2340004 | tf_op jit(solution)/shard_map/while
  133.0 1.1 copy-start.1
  138.2 0.7 copy-start.4
  138.2 3.1 %copy-start.11 = (f32[8]{0:T(128)S(1)}, f32[8]{0:T(128)}, u32[]{:S(2)}) copy-start(f32[8]{0:T(128)} %get-tuple-element.192) | copy-start | bytes 100 | tf_op jit(solution)/shard_map/while
  145.8 4.4 %copy-start.2 = (bf16[100,3900]{1,0:T(8,128)(2,1)S(1)}, bf16[100,3900]{1,0:T(8,128)(2,1)}, u32[]{:S(2)}) copy-start(bf16[100,3900]{1,0:T(8,128)(2,1)} %get-tuple-element.208) | copy-start | bytes 2340004 | tf_op jit(solution)/shard_map/while
  153.7 1.1 copy-start.1
  158.9 0.7 copy-start.4
  158.9 3.1 %copy-start.11 = (f32[8]{0:T(128)S(1)}, f32[8]{0:T(128)}, u32[]{:S(2)}) copy-start(f32[8]{0:T(128)} %get-tuple-element.192) | copy-start | bytes 100 | tf_op jit(solution)/shard_map/while
  162.1 0.5 copy-start.12
  166.5 4.4 %copy-start.2 = (bf16[100,3900]{1,0:T(8,128)(2,1)S(1)}, bf16[100,3900]{1,0:T(8,128)(2,1)}, u32[]{:S(2)}) copy-start(bf16[100,3900]{1,0:T(8,128)(2,1)} %get-tuple-element.208) | copy-start | bytes 2340004 | tf_op jit(solution)/shard_map/while
  174.3 1.1 copy-start.1
  179.5 0.7 copy-start.4
  179.6 3.1 %copy-start.11 = (f32[8]{0:T(128)S(1)}, f32[8]{0:T(128)}, u32[]{:S(2)}) copy-start(f32[8]{0:T(128)} %get-tuple-element.192) | copy-start | bytes 100 | tf_op jit(solution)/shard_map/while
  182.8 0.5 copy-start.12
  187.2 4.4 %copy-start.2 = (bf16[100,3900]{1,0:T(8,128)(2,1)S(1)}, bf16[100,3900]{1,0:T(8,128)(2,1)}, u32[]{:S(2)}) copy-start(bf16[100,3900]{1,0:T(8,128)(2,1)} %get-tuple-element.208) | copy-start | bytes 2340004 | tf_op jit(solution)/shard_map/while
  195.0 1.1 copy-start.1
  200.2 0.7 copy-start.4
  200.2 3.1 %copy-start.11 = (f32[8]{0:T(128)S(1)}, f32[8]{0:T(128)}, u32[]{:S(2)}) copy-start(f32[8]{0:T(128)} %get-tuple-element.192) | copy-start | bytes 100 | tf_op jit(solution)/shard_map/while
  216.9 1.1 copy-start.5
  216.9 1.2 copy-start.8
  (3 other events, 1.5 us)
Sparse Core Ops, SparseCore 0:
  218.2 53.0 all-reduce.4
where the time goes:
time: 285 us; the launch traced here: 282 us
  local copies, waits for them, and re-layouts  62.9 us (22%)
  matrix products  62.2 us (22%)
  blocking collectives  60.5 us (21%)
  other arithmetic  52.4 us (18%)
  loops' own time  15.5 us (5%)
  between operations  14.3 us (5%)
  starting transfers between devices  8.76 us (3%)
  waiting for transfers between devices  5.73 us (2%)
    psum x1, blocking collectives, local(): hot_grad = lax.psum(hot_local, ('group', 'shard')).astype(jnp.bfloat16)  53 us
    dot_general x24, matrix products, sample_pass(): jnp.einsum('hk,bhe->bke', weight, grad_low, preferred_element_type=jnp.fl...  33 us
    dot_general x24, matrix products, sample_pass(): jnp.einsum('hk,bke->bhe', weight, outer_rows, preferred_element_type=jnp....  29.2 us
    reshape x24, local copies, waits for them, and re-layouts, sample_pass(): grad_outer = grad_outer.reshape(batch_rows, below_maps, fields, breadth)  25.9 us
    another operation x1, loops' own time, local(): logits, gradients = lax.map(one_sample, (embedded, grad_logit))  15.5 us
    reduce_sum x24, other arithmetic, sample_pass(): jnp.sum(grad_outer * lower_state.astype(jnp.float32)[:, :, None, :], axis=1)  15.3 us
    dynamic_slice x8, local copies, waits for them, and re-layouts, local(): logits, gradients = lax.map(one_sample, (embedded, grad_logit))  10.6 us
    mul x8, other arithmetic, sample_pass(): grad_logit[:, None, None] * out_weight[section_index][None, :, None]  10.6 us
  transfers between devices with their start and end apart: 3, of which 2 were waited for; matrix products, arithmetic and copies ran while one was open for 2% of the time, Pallas kernels for 0%

commit v1 on v0

v1 whole, which is shorter than its diff:
```python
import functools

import jax
import jax.numpy as jnp
from jax import lax
from jax.experimental import pallas as pl
from jax.experimental.pallas import tpu as pltpu
from jax.sharding import PartitionSpec as P

BF = jnp.bfloat16
F32 = jnp.float32
MESH = pl.DeviceIdType.MESH
VMEM_LIMIT = 56 * 1024 * 1024


def up(value, unit):
    return (value + unit - 1) // unit * unit


def iota(shape, dim):
    return lax.broadcasted_iota(jnp.int32, shape, dim).astype(F32)


def dot(a, b):
    return jnp.dot(a, b, preferred_element_type=F32)


def dot_t(a, b):
    return lax.dot_general(a, b, (((0,), (0,)), ((), ())), preferred_element_type=F32)


def as_row(col, width):
    rows = col.shape[0]
    hit = iota((rows, width), 0) == iota((rows, width), 1)
    return jnp.sum(jnp.where(hit, col + 1.0, 0.0), axis=0, keepdims=True) - 1.0


def enter(me_g, me_s, n_g, n_s, groups):
    barrier = pltpu.get_barrier_semaphore()
    count = n_s - 1
    for k in range(1, n_s):
        pl.semaphore_signal(
            barrier, inc=1, device_id=(me_g, lax.rem(me_s + k, n_s)), device_id_type=MESH
        )
    if groups:
        count += n_g - 1
        for k in range(1, n_g):
            pl.semaphore_signal(
                barrier, inc=1, device_id=(lax.rem(me_g + k, n_g), me_s), device_id_type=MESH
            )
    pl.semaphore_wait(barrier, count)


def prepare_weight(w_ref, fields, maps_pad, fields_pad, wide, tall, wt_ref, wf_ref):
    high, cols = w_ref.shape
    cols_pad = up(cols, 128)
    total = fields_pad * maps_pad
    wide[...] = jnp.zeros_like(wide)
    wide[0:high, 0:cols] = w_ref[...].astype(F32)
    for b in range(cols_pad // 128):
        tall[b * 128 : (b + 1) * 128, :] = wide[:, b * 128 : (b + 1) * 128].T
    tall[cols_pad:, :] = jnp.zeros((tall.shape[0] - cols_pad, 128), F32)
    for f in range(fields_pad):
        block = slice(f * maps_pad, (f + 1) * maps_pad)
        if f < fields:
            wt_ref[block, :] = tall[pl.ds(f, maps_pad, stride=fields), :].astype(BF)
        else:
            wt_ref[block, :] = jnp.zeros((maps_pad, 128), BF)
    for b in range(total // 128):
        block = wt_ref[b * 128 : (b + 1) * 128, :].astype(F32).T
        wf_ref[:, b * 128 : (b + 1) * 128] = block[0 : wf_ref.shape[0]].astype(BF)


def lookup_kernel(
    n_g, n_s, cap,
    hot_row, cold_row, cold_owner, is_cold, hot_table, cold_table, w1, w2, w3, ow,
    emb, meta, wt1, wf1, wt2, wf2, wt3, wf3, owc,
    pack, wide, tall, ask, asked, reply, fetched, ask_s, ask_r, rep_s, rep_r,
):
    me_g, me_s = lax.axis_index("group"), lax.axis_index("shard")
    samples, fields = hot_row.shape
    fields_pad = up(fields, 8)
    looks = samples * fields_pad
    cap_pad = fetched.shape[1]
    slots = n_s * cap_pad
    hot_rows, shard_rows = hot_table.shape[0], cold_table.shape[0]

    pack[...] = jnp.full(pack.shape, -1.0, F32)
    for a, ref in enumerate((hot_row, cold_row, cold_owner, is_cold)):
        pack[a * samples : (a + 1) * samples, 0:fields] = ref[...].astype(F32)
    turned = pack[...].T

    def column(a):
        return jnp.concatenate(
            [
                turned[0:fields_pad, a * samples + s : a * samples + s + 1]
                for s in range(samples)
            ],
            axis=0,
        )

    hot_c, row_c, owner_c, flag_c = (column(a) for a in range(4))
    cold = flag_c == 1.0
    lanes = iota((looks, 128), 1)
    wanted = jnp.where(jnp.logical_and(owner_c == lanes, cold), 1.0, 0.0)
    lower = jnp.where(iota((looks, looks), 1) < iota((looks, looks), 0), 1.0, 0.0)
    earlier = dot(lower.astype(BF), wanted.astype(BF))
    pos_c = jnp.sum(earlier * wanted, axis=1, keepdims=True)
    target_c = jnp.where(cold, owner_c * cap_pad + pos_c, -1.0)
    at_pos = jnp.where(jnp.logical_and(pos_c == lanes, cold), 1.0, 0.0)
    code = row_c + 1.0
    code_hi = jnp.floor(code * (1.0 / 128.0))
    code_lo = code - code_hi * 128.0
    coded = jnp.concatenate([at_pos * code_hi, at_pos * code_lo], axis=1)
    found = dot_t(wanted.astype(BF), coded.astype(BF))
    ids = found[:, 0:128] * 128.0 + found[:, 128:256] - 1.0
    for o in range(n_s):
        ask[o] = jnp.broadcast_to(ids[o : o + 1, :], (8, 128))

    enter(me_g, me_s, n_g, n_s, False)

    def ask_copy(k):
        peer = lax.rem(me_s + k, n_s)
        return pltpu.make_async_remote_copy(
            src_ref=ask.at[peer], dst_ref=asked.at[me_s], send_sem=ask_s.at[k],
            recv_sem=ask_r.at[k], device_id=(me_g, peer), device_id_type=MESH,
        )

    def ask_wait(k):
        src = lax.rem(me_s + n_s - k, n_s)
        return pltpu.make_async_remote_copy(
            src_ref=ask.at[src], dst_ref=asked.at[src], send_sem=ask_s.at[k],
            recv_sem=ask_r.at[k], device_id=(me_g, src), device_id_type=MESH,
        )

    for k in range(1, n_s):
        ask_copy(k).start()
    asked[me_s] = ask[me_s]

    at_hot = jnp.logical_and(hot_c == iota((looks, hot_rows), 1), jnp.logical_not(cold))
    hot_part = dot(jnp.where(at_hot, 1.0, 0.0).astype(BF), hot_table[...])
    prepare_weight(w1, fields, wt1.shape[0] // fields_pad, fields_pad, wide, tall, wt1, wf1)

    for k in range(1, n_s):
        ask_wait(k).wait_recv()
    pack[...] = jnp.full(pack.shape, -1.0, F32)
    for d in range(n_s):
        pack[d : d + 1, :] = asked[d][0:1, :]
    turned2 = pack[...].T
    ids_c = jnp.concatenate([turned2[0:cap_pad, d : d + 1] for d in range(n_s)], axis=0)
    at_row = jnp.where(ids_c == iota((slots, shard_rows), 1), 1.0, 0.0)
    rows = dot(at_row.astype(BF), cold_table[...]).astype(BF)
    for d in range(n_s):
        reply[d] = rows[d * cap_pad : (d + 1) * cap_pad]

    def rep_copy(k):
        peer = lax.rem(me_s + k, n_s)
        return pltpu.make_async_remote_copy(
            src_ref=reply.at[peer], dst_ref=fetched.at[me_s], send_sem=rep_s.at[k],
            recv_sem=rep_r.at[k], device_id=(me_g, peer), device_id_type=MESH,
        )

    def rep_wait(k):
        src = lax.rem(me_s + n_s - k, n_s)
        return pltpu.make_async_remote_copy(
            src_ref=reply.at[src], dst_ref=fetched.at[src], send_sem=rep_s.at[k],
            recv_sem=rep_r.at[k], device_id=(me_g, src), device_id_type=MESH,
        )

    for k in range(1, n_s):
        rep_copy(k).start()
    fetched[me_s] = reply[me_s]

    prepare_weight(w2, fields, wt2.shape[0] // fields_pad, fields_pad, wide, tall, wt2, wf2)
    prepare_weight(w3, fields, wt3.shape[0] // fields_pad, fields_pad, wide, tall, wt3, wf3)
    width = meta.shape[1]
    meta[...] = jnp.full(meta.shape, -1.0, F32)
    meta[0:1, :] = as_row(jnp.where(cold, -1.0, hot_c), width)
    meta[1:2, :] = as_row(target_c, width)
    meta[2:3, :] = as_row(ids_c, width)
    pack[...] = jnp.zeros(pack.shape, F32)
    pack[0 : ow.shape[0], 0 : ow.shape[1]] = ow[...]
    owc[...] = pack[...].T

    for k in range(1, n_s):
        rep_wait(k).wait_recv()
    at_slot = jnp.where(target_c == iota((looks, slots), 1), 1.0, 0.0).astype(BF)
    got = jnp.concatenate([fetched[d] for d in range(n_s)], axis=0)
    emb[...] = (dot(at_slot, got) + hot_part).astype(BF)
    for k in range(1, n_s):
        ask_copy(k).wait_send()
        rep_copy(k).wait_send()


def layers_kernel(
    fields, gl, emb, wt1, wf1, wt2, wf2, wt3, wf3, owc,
    grad, logit, outer, base, low, states, ge,
):
    fields_pad = base.shape[0]
    samples = emb.shape[0] // fields_pad
    pair = base.shape[1] // 128
    high = wf1.shape[0]
    wts, wfs = (wt1, wt2, wt3), (wf1, wf2, wf3)

    @pl.loop(0, samples // pair)
    def _(b):
        row0 = pl.multiple_of(b * (pair * fields_pad), 8)
        block = emb[pl.ds(row0, pair * fields_pad), :].astype(F32)
        x0 = jnp.concatenate(
            [block[p * fields_pad : (p + 1) * fields_pad] for p in range(pair)], axis=1
        )
        base[...] = x0
        lanes = base.shape[1]
        grow = jnp.concatenate(
            [jnp.full((1, 128), gl[b * pair + p], F32) for p in range(pair)], axis=1
        )
        first_pad = wt1.shape[0] // fields_pad
        low[0:fields_pad, :] = x0
        low[fields_pad:first_pad, :] = jnp.zeros((first_pad - fields_pad, lanes), F32)
        below = low[...]
        inputs = [below]
        total = jnp.zeros((1, lanes), F32)
        for k in range(3):
            maps_pad = wts[k].shape[0] // fields_pad
            below_b = below.astype(BF)
            for f in range(fields_pad):
                start = f * maps_pad
                if f < fields:
                    wide = jnp.broadcast_to(base[f : f + 1, :], (16, lanes)).astype(BF)
                    for t in range(maps_pad // 16):
                        outer[start + t * 16 : start + t * 16 + 16, :] = (
                            below_b[t * 16 : t * 16 + 16] * wide
                        )
                else:
                    outer[start : start + maps_pad, :] = jnp.zeros((maps_pad, lanes), BF)
            depth = fields_pad * maps_pad
            state = dot(wfs[k][...], outer[0:depth, :]).astype(BF).astype(F32)
            total = total + jnp.sum(state * owc[0:high, k : k + 1], axis=0, keepdims=True)
            states[k] = state
            below = state
        for p in range(pair):
            one = jnp.sum(total[:, p * 128 : (p + 1) * 128], axis=1, keepdims=True)
            logit[pl.ds(b * pair + p, 1), :] = jnp.broadcast_to(one, (1, 128))

        carried = jnp.zeros((high, lanes), F32)
        chunk = 8
        for k in (2, 1, 0):
            maps_pad = wts[k].shape[0] // fields_pad
            used = maps_pad - 8
            grad_state = carried + owc[0:high, k : k + 1] * grow
            grad_low = jnp.concatenate(
                [grad_state.astype(BF), jnp.zeros((128 - high, lanes), BF)], axis=0
            )
            lower = low if k == 0 else states.at[k - 1]
            acc = jnp.zeros((used, lanes), F32)
            for c in range(0, fields, chunk):
                many = min(chunk, fields_pad - c)
                g = dot(wts[k][c * maps_pad : (c + many) * maps_pad, :], grad_low)
                for f in range(c, min(c + many, fields)):
                    gf = g[(f - c) * maps_pad : (f - c) * maps_pad + used]
                    acc = acc + gf * base[f : f + 1, :]
                    part = jnp.sum(gf * lower[0:used, :], axis=0, keepdims=True)
                    if k == 2:
                        ge[f : f + 1, :] = part
                    else:
                        ge[f : f + 1, :] += part
            if k > 0:
                carried = jnp.concatenate(
                    [acc, jnp.zeros((high - used, lanes), F32)], axis=0
                )
            else:
                carried = acc
        out = ge[...] + carried[0:fields_pad]
        keep = lax.broadcasted_iota(jnp.int32, out.shape, 0) < fields
        out = jnp.where(keep, out, 0.0).astype(BF)
        grad[pl.ds(row0, pair * fields_pad), :] = jnp.concatenate(
            [out[:, p * 128 : (p + 1) * 128] for p in range(pair)], axis=0
        )


def grads_kernel(
    n_g, n_s, cap_pad, grad, meta,
    hot_out, cold_out,
    send, inc, allin, ids, hot_part, hot_in, hot_mid, hot_all,
    send_s, send_r, all_s, all_r, id_s, id_r, hs_s, hs_r, hm_s, hm_r, hg_s, hg_r,
):
    me_g, me_s = lax.axis_index("group"), lax.axis_index("shard")
    looks = grad.shape[0]
    slots = n_s * cap_pad
    hot_rows, shard_rows = hot_out.shape[0], cold_out.shape[0]
    part = hot_rows // n_s

    def shard_copy(k, src, dst, s_sem, r_sem):
        peer = lax.rem(me_s + k, n_s)
        return pltpu.make_async_remote_copy(
            src_ref=src(peer), dst_ref=dst(me_s), send_sem=s_sem.at[k],
            recv_sem=r_sem.at[k], device_id=(me_g, peer), device_id_type=MESH,
        )

    def shard_wait(k, src, dst, s_sem, r_sem):
        peer = lax.rem(me_s + n_s - k, n_s)
        return pltpu.make_async_remote_copy(
            src_ref=src(peer), dst_ref=dst(peer), send_sem=s_sem.at[k],
            recv_sem=r_sem.at[k], device_id=(me_g, peer), device_id_type=MESH,
        )

    def group_copy(k, src, dst, s_sem, r_sem):
        peer = lax.rem(me_g + k, n_g)
        return pltpu.make_async_remote_copy(
            src_ref=src, dst_ref=dst(me_g), send_sem=s_sem.at[k],
            recv_sem=r_sem.at[k], device_id=(peer, me_s), device_id_type=MESH,
        )

    def group_wait(k, src, dst, s_sem, r_sem):
        peer = lax.rem(me_g + n_g - k, n_g)
        return pltpu.make_async_remote_copy(
            src_ref=src, dst_ref=dst(peer), send_sem=s_sem.at[k],
            recv_sem=r_sem.at[k], device_id=(peer, me_s), device_id_type=MESH,
        )

    cold_x = (lambda p: send.at[p], lambda p: inc.at[p], send_s, send_r)
    cold_g = (inc, lambda p: allin.at[p], all_s, all_r)
    id_g = (meta, lambda p: ids.at[p], id_s, id_r)
    hot_x = (lambda p: hot_part.at[p], lambda p: hot_in.at[p], hs_s, hs_r)
    hot_g = (hot_mid, lambda p: hot_all.at[p], hm_s, hm_r)

    def hot_slice(p):
        return hot_out.at[pl.ds(pl.multiple_of(p * part, part), part)]

    hot_f = (lambda p: hot_slice(me_s), hot_slice, hg_s, hg_r)

    g = grad[...]
    at_slot = jnp.where(meta[1:2, 0:looks] == iota((slots, looks), 0), 1.0, 0.0)
    out = dot(at_slot.astype(BF), g).astype(BF)
    for d in range(n_s):
        send[d] = out[d * cap_pad : (d + 1) * cap_pad]

    enter(me_g, me_s, n_g, n_s, True)
    for k in range(1, n_s):
        shard_copy(k, *cold_x).start()
    for k in range(1, n_g):
        group_copy(k, *id_g).start()
    inc[me_s] = send[me_s]
    ids[me_g] = meta[...]

    at_hot = jnp.where(meta[0:1, 0:looks] == iota((hot_rows, looks), 0), 1.0, 0.0)
    hots = dot(at_hot.astype(BF), g).astype(BF)
    for d in range(n_s):
        hot_part[d] = hots[d * part : (d + 1) * part]
    for k in range(1, n_s):
        shard_copy(k, *hot_x).start()
    hot_in[me_s] = hot_part[me_s]

    for k in range(1, n_s):
        shard_wait(k, *cold_x).wait_recv()
    for k in range(1, n_g):
        group_copy(k, *cold_g).start()
    allin[me_g] = inc[...]

    for k in range(1, n_s):
        shard_wait(k, *hot_x).wait_recv()
    total = hot_in[0].astype(F32)
    for d in range(1, n_s):
        total = total + hot_in[d].astype(F32)
    hot_mid[...] = total.astype(BF)
    for k in range(1, n_g):
        group_copy(k, *hot_g).start()
    hot_all[me_g] = hot_mid[...]

    for k in range(1, n_g):
        group_wait(k, *hot_g).wait_recv()
    total = hot_all[0].astype(F32)
    for d in range(1, n_g):
        total = total + hot_all[d].astype(F32)
    hot_slice(me_s)[...] = total.astype(BF)
    for k in range(1, n_s):
        shard_copy(k, *hot_f).start()

    for k in range(1, n_g):
        group_wait(k, *id_g).wait_recv()
        group_wait(k, *cold_g).wait_recv()
    terms = jnp.concatenate(
        [allin[q, d] for q in range(n_g) for d in range(n_s)], axis=0
    )
    step = 512 if shard_rows % 512 == 0 else shard_rows

    @pl.loop(0, shard_rows // step)
    def _(t):
        first = pl.multiple_of(t * step, step)
        here = iota((step, slots), 0) + first.astype(F32)
        at = jnp.concatenate(
            [
                jnp.where(ids[q][2:3, 0:slots] == here, 1.0, 0.0).astype(BF)
                for q in range(n_g)
            ],
            axis=1,
        )
        cold_out[pl.ds(first, step), :] = dot(at, terms).astype(BF)

    for k in range(1, n_s):
        shard_wait(k, *hot_f).wait_recv()
    for k in range(1, n_s):
        shard_copy(k, *cold_x).wait_send()
        shard_copy(k, *hot_x).wait_send()
        shard_copy(k, *hot_f).wait_send()
    for k in range(1, n_g):
        group_copy(k, *id_g).wait_send()
        group_copy(k, *cold_g).wait_send()
        group_copy(k, *hot_g).wait_send()


def local(
    hot_row, cold_row, cold_owner, is_cold, grad_logit, hot_table, cold_table,
    first_weight, second_weight, third_weight, out_weight,
):
    n_g, n_s = lax.axis_size("group"), lax.axis_size("shard")
    samples, fields = hot_row.shape
    breadth = hot_table.shape[1]
    maps = out_weight.shape[1]
    cap = samples * fields // n_s
    cap_pad = up(cap, 16)
    slots = n_s * cap_pad
    fields_pad = up(fields, 8)
    looks = samples * fields_pad
    first_pad, maps_pad = up(fields_pad, 16), up(maps, 16)
    depth1, depth2 = fields_pad * first_pad, fields_pad * maps_pad
    wide = up(max(slots, looks), 128)
    vm = pl.BlockSpec(memory_space=pltpu.VMEM)
    sd = jax.ShapeDtypeStruct
    dma = pltpu.SemaphoreType.DMA

    emb, meta, wt1, wf1, wt2, wf2, wt3, wf3, owc = pl.pallas_call(
        functools.partial(lookup_kernel, n_g, n_s, cap),
        out_shape=(
            sd((looks, breadth), BF), sd((8, wide), F32),
            sd((depth1, 128), BF), sd((maps_pad, depth1), BF),
            sd((depth2, 128), BF), sd((maps_pad, depth2), BF),
            sd((depth2, 128), BF), sd((maps_pad, depth2), BF),
            sd((128, 128), F32),
        ),
        in_specs=[vm] * 10,
        out_specs=tuple([vm] * 9),
        scratch_shapes=[
            pltpu.VMEM((128, 128), F32),
            pltpu.VMEM((128, up(second_weight.shape[1], 128)), F32),
            pltpu.VMEM((depth2, 128), F32),
            pltpu.VMEM((n_s, 8, 128), F32),
            pltpu.VMEM((n_s, 8, 128), F32),
            pltpu.VMEM((n_s, cap_pad, breadth), BF),
            pltpu.VMEM((n_s, cap_pad, breadth), BF),
            dma((n_s,)), dma((n_s,)), dma((n_s,)), dma((n_s,)),
        ],
        compiler_params=pltpu.CompilerParams(
            collective_id=0, has_side_effects=True, vmem_limit_bytes=VMEM_LIMIT
        ),
        name="lookup",
    )(
        hot_row, cold_row, cold_owner, is_cold, hot_table, cold_table,
        first_weight, second_weight, third_weight, out_weight,
    )

    pair = 2
    lanes = pair * 128
    grad, logit = pl.pallas_call(
        functools.partial(layers_kernel, fields),
        out_shape=(sd((looks, breadth), BF), sd((samples, 128), F32)),
        in_specs=[pl.BlockSpec(memory_space=pltpu.SMEM)] + [vm] * 8,
        out_specs=(vm, vm),
        scratch_shapes=[
            pltpu.VMEM((depth2, lanes), BF),
            pltpu.VMEM((fields_pad, lanes), F32),
            pltpu.VMEM((first_pad, lanes), F32),
            pltpu.VMEM((3, maps_pad, lanes), F32),
            pltpu.VMEM((fields_pad, lanes), F32),
        ],
        compiler_params=pltpu.CompilerParams(vmem_limit_bytes=VMEM_LIMIT),
        name="layers",
    )(grad_logit, emb, wt1, wf1, wt2, wf2, wt3, wf3, owc)

    part = hot_table.shape[0] // n_s
    hot_grad, cold_grad = pl.pallas_call(
        functools.partial(grads_kernel, n_g, n_s, cap_pad),
        out_shape=(sd(hot_table.shape, BF), sd(cold_table.shape, BF)),
        in_specs=[vm, vm],
        out_specs=(vm, vm),
        scratch_shapes=[
            pltpu.VMEM((n_s, cap_pad, breadth), BF),
            pltpu.VMEM((n_s, cap_pad, breadth), BF),
            pltpu.VMEM((n_g, n_s, cap_pad, breadth), BF),
            pltpu.VMEM((n_g, 8, wide), F32),
            pltpu.VMEM((n_s, part, breadth), BF),
            pltpu.VMEM((n_s, part, breadth), BF),
            pltpu.VMEM((part, breadth), BF),
            pltpu.VMEM((n_g, part, breadth), BF),
            dma((n_s,)), dma((n_s,)), dma((n_g,)), dma((n_g,)), dma((n_g,)), dma((n_g,)),
            dma((n_s,)), dma((n_s,)), dma((n_g,)), dma((n_g,)), dma((n_s,)), dma((n_s,)),
        ],
        compiler_params=pltpu.CompilerParams(
            collective_id=1, has_side_effects=True, vmem_limit_bytes=VMEM_LIMIT
        ),
        name="grads",
    )(grad, meta)
    return hot_grad, cold_grad, logit[:, 0]


def solution(mesh):
    rows = P(("group", "shard"), None)
    return jax.shard_map(
        local,
        mesh=mesh,
        in_specs=(
            rows, rows, rows, rows, P(("group", "shard")), P(), P("shard", None),
            P(), P(), P(), P(),
        ),
        out_specs=(P(), P("shard", None), P(("group", "shard"))),
        check_vma=False,
    )
```

time: 285 us -> 72.7 us (0.26)
  Pallas kernels: 0 us -> 66.8 us
  matrix products: 62.2 us -> 0 us
  blocking collectives: 60.5 us -> 0 us
  local copies, waits for them, and re-layouts: 62.9 us -> 4.24 us
  other arithmetic: 52.4 us -> 0 us
  loops' own time: 15.5 us -> 0 us
  between operations: 14.3 us -> 0.66 us
  starting transfers between devices: 8.76 us -> 0 us
  waiting for transfers between devices: 5.73 us -> 0 us
    pallas_call x0 -> x3, Pallas kernels: none -> 66.8 us  [the longest x1 30.9 us: local(): pl.pallas_call(functools.partial(grads_kernel, n_g, n_s, cap_pad), out_sh...]
    dot_general x48 -> x0, matrix products: 62.2 us -> none  [the longest x24 33 us: sample_pass(): jnp.einsum('hk,bhe->bke', weight, grad_low, preferred_element_type=jnp.fl...]
    psum x1 -> x0, blocking collectives: 53 us -> none  [local(): hot_grad = lax.psum(hot_local, ('group', 'shard')).astype(jnp.bfloat16)]
    reshape x29 -> x0, local copies, waits for them, and re-layouts: 28.4 us -> none  [the longest x24 25.9 us: sample_pass(): grad_outer = grad_outer.reshape(batch_rows, below_maps, fields, breadth)]
    mul x17 -> x0, other arithmetic: 16.9 us -> none  [the longest x8 10.6 us: sample_pass(): grad_logit[:, None, None] * out_weight[section_index][None, :, None]]
    another operation x1 -> x0, loops' own time: 15.5 us -> none  [local(): logits, gradients = lax.map(one_sample, (embedded, grad_logit))]
    reduce_sum x25 -> x0, other arithmetic: 15.3 us -> none  [the longest x24 15.3 us: sample_pass(): jnp.sum(grad_outer * lower_state.astype(jnp.float32)[:, :, None, :], axis=1)]
    dynamic_slice x8 -> x0, local copies, waits for them, and re-layouts: 10.6 us -> none  [local(): logits, gradients = lax.map(one_sample, (embedded, grad_logit))]
  transfers between devices with their start and end apart: 3 -> 0, of which waited for: 2 -> 0; matrix products, arithmetic and copies ran while one was open for 2% -> 0% of each run, Pallas kernels for 0% -> 0%
where the time goes in v1:
time: 72.7 us; the launch traced here: 71.7 us
  Pallas kernels  66.8 us (92%)
  local copies, waits for them, and re-layouts  4.24 us (6%)
    pallas_call x1, Pallas kernels, local(): pl.pallas_call(functools.partial(grads_kernel, n_g, n_s, cap_pad), out_sh...  30.9 us
    pallas_call x1, Pallas kernels, local(): pl.pallas_call(functools.partial(layers_kernel, fields), out_shape=(sd((l...  18.4 us
    pallas_call x1, Pallas kernels, local(): pl.pallas_call(functools.partial(lookup_kernel, n_g, n_s, cap), out_shape...  17.5 us
    unnamed x4, local copies, waits for them, and re-layouts  2.93 us

profile of v1, /device:TPU:0, one launch (start us, length us, event | category | flops | bytes accessed | tf_op | source)
XLA Modules:
  0.0 71.7 jit_solution(1074574928510049030)
XLA Ops:
  0.6 17.5 %lookup.1 = (bf16[320,128]{1,0:T(8,128)(2,1)}, f32[8,384]{1,0:T(8,128)}, bf16[1920,128]{1,0:T(8,128)(2,1)}, bf16[112,1920]{1,0:T(8,128)(2,1)}, bf16[4480,128]{1,...) custom-call(s32[8,39]{1,0:T(8,128)} %hot_row.1, ...), custom_call_target="tpu_custom_call" | custom-call | tf_op jit(solution)/shard_map/lookup/pallas_call | solution.py:432
  18.2 18.4 %layers.1 = (bf16[320,128]{1,0:T(8,128)(2,1)}, f32[8,128]{1,0:T(8,128)}) custom-call(f32[8]{0:T(128)} %gl.1, bf16[320,128]{1,0:T(8,128)(2,1)} %get-tuple-element.16.emb, bf16[1920,128]{1,0:T(8,128)(2,1)} %get-tuple-element.17.wt1, bf16[112,1920]{1,0:T(8,128)(2,1)} %get-tuple-element.18.wf1, bf16[4480,128]{1,0:T(8,128)(2,1)} %get-tuple-element.19.wt2, ...), custom_call_target="tpu_custom_call" | custom-call | tf_op jit(solution)/shard_map/layers/pallas_call | solution.py:464
  36.6 1.3 %slice_reduce_fusion = f32[8]{0:T(128)} fusion(f32[8,128]{1,0:T(8,128)} %get-tuple-element.28), kind=kLoop, calls=%fused_computation | loop fusion | bytes 64 | tf_op jit(solution)/shard_map/slice | solution.py:503
  37.9 30.9 %grads.1 = (bf16[2048,128]{1,0:T(8,128)(2,1)}, bf16[4096,128]{1,0:T(8,128)(2,1)}) custom-call(bf16[320,128]{1,0:T(8,128)(2,1)} %get-tuple-element.24.grad, f32[8,384]{1,0:T(8,128)} %get-tuple-element.25.meta), custom_call_target="tpu_custom_call" | custom-call | tf_op jit(solution)/shard_map/grads/pallas_call | solution.py:481
  68.8 0.0 copy-start
  68.8 2.0 %copy.16 = bf16[2048,128]{1,0:T(8,128)(2,1)} copy(bf16[2048,128]{1,0:T(8,128)(2,1)} %get-tuple-element.32) | data formatting | bytes 1048576
  70.8 0.0 copy-done
  70.8 1.0 %copy.17 = bf16[4096,128]{1,0:T(8,128)(2,1)} copy(bf16[4096,128]{1,0:T(8,128)(2,1)S(1)} %copy-done) | data formatting | bytes 2097152
Async XLA Ops:
  68.8 2.0 %copy-start = (bf16[4096,128]{1,0:T(8,128)(2,1)S(1)}, bf16[4096,128]{1,0:T(8,128)(2,1)}, u32[]{:S(2)}) copy-start(bf16[4096,128]{1,0:T(8,128)(2,1)} %get-tuple-element.33) | copy-start | bytes 3145732

commit v2 on v1

v2 whole, which is shorter than its diff:
```python
import functools

import jax
import jax.numpy as jnp
from jax import lax
from jax.experimental import pallas as pl
from jax.experimental.pallas import tpu as pltpu
from jax.sharding import PartitionSpec as P

BF = jnp.bfloat16
F32 = jnp.float32
MESH = pl.DeviceIdType.MESH
VMEM_LIMIT = 56 * 1024 * 1024


def up(value, unit):
    return (value + unit - 1) // unit * unit


def iota(shape, dim):
    return lax.broadcasted_iota(jnp.int32, shape, dim).astype(F32)


def dot(a, b):
    return jnp.dot(a, b, preferred_element_type=F32)


def dot_t(a, b):
    return lax.dot_general(a, b, (((0,), (0,)), ((), ())), preferred_element_type=F32)


def as_row(col, width):
    rows = col.shape[0]
    hit = iota((rows, width), 0) == iota((rows, width), 1)
    return jnp.sum(jnp.where(hit, col + 1.0, 0.0), axis=0, keepdims=True) - 1.0


def prepare_weight(w_ref, fields, maps_pad, fields_pad, wide, tall, wt_ref, wf_ref):
    high, cols = w_ref.shape
    cols_pad = up(cols, 128)
    total = fields_pad * maps_pad
    wide[...] = jnp.zeros_like(wide)
    wide[0:high, 0:cols] = w_ref[...].astype(F32)
    for b in range(cols_pad // 128):
        tall[b * 128 : (b + 1) * 128, :] = wide[:, b * 128 : (b + 1) * 128].T
    tall[cols_pad:, :] = jnp.zeros((tall.shape[0] - cols_pad, 128), F32)
    for f in range(fields_pad):
        block = slice(f * maps_pad, (f + 1) * maps_pad)
        if f < fields:
            wt_ref[block, :] = tall[pl.ds(f, maps_pad, stride=fields), :].astype(BF)
        else:
            wt_ref[block, :] = jnp.zeros((maps_pad, 128), BF)
    for b in range(total // 128):
        block = wt_ref[b * 128 : (b + 1) * 128, :].astype(F32).T
        wf_ref[:, b * 128 : (b + 1) * 128] = block[0 : wf_ref.shape[0]].astype(BF)


def step_kernel(
    n_g, n_s,
    hot_row, cold_row, cold_owner, is_cold, gl, hot_table, cold_table, w1, w2, w3, ow,
    hot_out, cold_out, logit,
    hot_v, cold_v, w1_v, w2_v, w3_v, emb, wt1, wf1, wt2, wf2, wt3, wf3, owc, meta,
    pack, wide, tall, ask, asked, reply, fetched,
    outer, base, low, states, ge,
    gmine, gall, inc, allin, ids_all, hot_mid, hot_all,
    load_s, ask_s, ask_r, rep_s, rep_r, sp_s, sp_r,
    all_s, all_r, id_s, id_r, hm_s, hm_r, hg_s, hg_r,
):
    me_g, me_s = lax.axis_index("group"), lax.axis_index("shard")
    barrier = pltpu.get_barrier_semaphore()
    for k in range(1, n_s):
        pl.semaphore_signal(
            barrier, inc=1, device_id=(me_g, lax.rem(me_s + k, n_s)), device_id_type=MESH
        )
    for k in range(1, n_g):
        pl.semaphore_signal(
            barrier, inc=1, device_id=(lax.rem(me_g + k, n_g), me_s), device_id_type=MESH
        )
    loads = [
        pltpu.make_async_copy(src, dst, load_s.at[i])
        for i, (src, dst) in enumerate(
            ((hot_table, hot_v), (cold_table, cold_v), (w1, w1_v), (w2, w2_v), (w3, w3_v))
        )
    ]
    for load in loads:
        load.start()
    samples, fields = hot_row.shape
    fields_pad = up(fields, 8)
    looks = samples * fields_pad
    cap_pad = fetched.shape[1]
    slots = n_s * cap_pad
    hot_rows, shard_rows = hot_out.shape[0], cold_out.shape[0]
    part = hot_rows // n_s
    pair = base.shape[1] // 128
    high = wf1.shape[0]
    wts, wfs = (wt1, wt2, wt3), (wf1, wf2, wf3)

    def shard_copy(k, src, dst, s_sem, r_sem):
        peer = lax.rem(me_s + k, n_s)
        return pltpu.make_async_remote_copy(
            src_ref=src(peer), dst_ref=dst(me_s), send_sem=s_sem.at[k],
            recv_sem=r_sem.at[k], device_id=(me_g, peer), device_id_type=MESH,
        )

    def shard_wait(k, src, dst, s_sem, r_sem):
        peer = lax.rem(me_s + n_s - k, n_s)
        return pltpu.make_async_remote_copy(
            src_ref=src(peer), dst_ref=dst(peer), send_sem=s_sem.at[k],
            recv_sem=r_sem.at[k], device_id=(me_g, peer), device_id_type=MESH,
        )

    def group_copy(k, src, dst, s_sem, r_sem):
        peer = lax.rem(me_g + k, n_g)
        return pltpu.make_async_remote_copy(
            src_ref=src, dst_ref=dst(me_g), send_sem=s_sem.at[k],
            recv_sem=r_sem.at[k], device_id=(peer, me_s), device_id_type=MESH,
        )

    def group_wait(k, src, dst, s_sem, r_sem):
        peer = lax.rem(me_g + n_g - k, n_g)
        return pltpu.make_async_remote_copy(
            src_ref=src, dst_ref=dst(peer), send_sem=s_sem.at[k],
            recv_sem=r_sem.at[k], device_id=(peer, me_s), device_id_type=MESH,
        )

    cold_g = (inc, lambda p: allin.at[p], all_s, all_r)
    id_g = (meta, lambda p: ids_all.at[p], id_s, id_r)
    hot_g = (hot_mid, lambda p: hot_all.at[p], hm_s, hm_r)

    def hot_slice(p):
        return hot_out.at[pl.ds(pl.multiple_of(p * part, part), part)]

    hot_f = (lambda p: hot_slice(me_s), hot_slice, hg_s, hg_r)

    def spread_copy(b, k):
        peer = lax.rem(me_s + k, n_s)
        return pltpu.make_async_remote_copy(
            src_ref=gmine.at[b], dst_ref=gall.at[me_s, b], send_sem=sp_s.at[b, k],
            recv_sem=sp_r.at[b, k], device_id=(me_g, peer), device_id_type=MESH,
        )

    def spread_wait(b, k):
        src = lax.rem(me_s + n_s - k, n_s)
        return pltpu.make_async_remote_copy(
            src_ref=gmine.at[b], dst_ref=gall.at[src, b], send_sem=sp_s.at[b, k],
            recv_sem=sp_r.at[b, k], device_id=(me_g, src), device_id_type=MESH,
        )

    pack[...] = jnp.full(pack.shape, -1.0, F32)
    for a, ref in enumerate((hot_row, cold_row, cold_owner, is_cold)):
        pack[a * samples : (a + 1) * samples, 0:fields] = ref[...].astype(F32)
    turned = pack[...].T

    def column(a):
        return jnp.concatenate(
            [
                turned[0:fields_pad, a * samples + s : a * samples + s + 1]
                for s in range(samples)
            ],
            axis=0,
        )

    hot_c, row_c, owner_c, flag_c = (column(a) for a in range(4))
    cold = flag_c == 1.0
    lanes = iota((looks, 128), 1)
    wanted = jnp.where(jnp.logical_and(owner_c == lanes, cold), 1.0, 0.0)
    lower = jnp.where(iota((looks, looks), 1) < iota((looks, looks), 0), 1.0, 0.0)
    earlier = dot(lower.astype(BF), wanted.astype(BF))
    pos_c = jnp.sum(earlier * wanted, axis=1, keepdims=True)
    target_c = jnp.where(cold, owner_c * cap_pad + pos_c, -1.0)
    at_pos = jnp.where(jnp.logical_and(pos_c == lanes, cold), 1.0, 0.0)
    code = row_c + 1.0
    code_hi = jnp.floor(code * (1.0 / 128.0))
    code_lo = code - code_hi * 128.0
    coded = jnp.concatenate([at_pos * code_hi, at_pos * code_lo], axis=1)
    found = dot_t(wanted.astype(BF), coded.astype(BF))
    ids = found[:, 0:128] * 128.0 + found[:, 128:256] - 1.0
    width = meta.shape[1]
    hot_r = as_row(jnp.where(cold, -1.0, hot_c), width)
    target_r = as_row(target_c, width)
    for o in range(n_s):
        ask[o, 0:1, 0:128] = ids[o : o + 1, :]
        ask[o, 1:2, :] = hot_r
        ask[o, 2:3, :] = target_r

    pl.semaphore_wait(barrier, n_s - 1 + n_g - 1)

    def ask_copy(k):
        peer = lax.rem(me_s + k, n_s)
        return pltpu.make_async_remote_copy(
            src_ref=ask.at[peer], dst_ref=asked.at[me_s], send_sem=ask_s.at[k],
            recv_sem=ask_r.at[k], device_id=(me_g, peer), device_id_type=MESH,
        )

    def ask_wait(k):
        src = lax.rem(me_s + n_s - k, n_s)
        return pltpu.make_async_remote_copy(
            src_ref=ask.at[src], dst_ref=asked.at[src], send_sem=ask_s.at[k],
            recv_sem=ask_r.at[k], device_id=(me_g, src), device_id_type=MESH,
        )

    for k in range(1, n_s):
        ask_copy(k).start()
    asked[me_s] = ask[me_s]

    loads[0].wait()
    at_hot = jnp.logical_and(hot_c == iota((looks, hot_rows), 1), jnp.logical_not(cold))
    hot_part = dot(jnp.where(at_hot, 1.0, 0.0).astype(BF), hot_v[...])
    loads[2].wait()
    prepare_weight(w1_v, fields, wt1.shape[0] // fields_pad, fields_pad, wide, tall, wt1, wf1)

    for k in range(1, n_s):
        ask_wait(k).wait_recv()
    pack[...] = jnp.full(pack.shape, -1.0, F32)
    for d in range(n_s):
        pack[d : d + 1, :] = asked[d, 0:1, 0:128]
    turned2 = pack[...].T
    ids_c = jnp.concatenate([turned2[0:cap_pad, d : d + 1] for d in range(n_s)], axis=0)
    at_row = jnp.where(ids_c == iota((slots, shard_rows), 1), 1.0, 0.0)
    loads[1].wait()
    rows = dot(at_row.astype(BF), cold_v[...]).astype(BF)
    for d in range(n_s):
        reply[d] = rows[d * cap_pad : (d + 1) * cap_pad]

    def rep_copy(k):
        peer = lax.rem(me_s + k, n_s)
        return pltpu.make_async_remote_copy(
            src_ref=reply.at[peer], dst_ref=fetched.at[me_s], send_sem=rep_s.at[k],
            recv_sem=rep_r.at[k], device_id=(me_g, peer), device_id_type=MESH,
        )

    def rep_wait(k):
        src = lax.rem(me_s + n_s - k, n_s)
        return pltpu.make_async_remote_copy(
            src_ref=reply.at[src], dst_ref=fetched.at[src], send_sem=rep_s.at[k],
            recv_sem=rep_r.at[k], device_id=(me_g, src), device_id_type=MESH,
        )

    for k in range(1, n_s):
        rep_copy(k).start()
    fetched[me_s] = reply[me_s]

    meta[...] = jnp.broadcast_to(as_row(ids_c, width), meta.shape)
    for k in range(1, n_g):
        group_copy(k, *id_g).start()
    ids_all[me_g] = meta[...]
    loads[3].wait()
    prepare_weight(w2_v, fields, wt2.shape[0] // fields_pad, fields_pad, wide, tall, wt2, wf2)
    loads[4].wait()
    prepare_weight(w3_v, fields, wt3.shape[0] // fields_pad, fields_pad, wide, tall, wt3, wf3)
    pack[...] = jnp.zeros(pack.shape, F32)
    pack[0 : ow.shape[0], 0 : ow.shape[1]] = ow[...]
    owc[...] = pack[...].T

    for k in range(1, n_s):
        rep_wait(k).wait_recv()
    at_slot = jnp.where(target_c == iota((looks, slots), 1), 1.0, 0.0).astype(BF)
    got = jnp.concatenate([fetched[d] for d in range(n_s)], axis=0)
    emb[...] = (dot(at_slot, got) + hot_part).astype(BF)
    for k in range(1, n_s):
        ask_copy(k).wait_send()
        rep_copy(k).wait_send()

    @pl.loop(0, samples // pair)
    def _(b):
        row0 = pl.multiple_of(b * (pair * fields_pad), 8)
        block = emb[pl.ds(row0, pair * fields_pad), :].astype(F32)
        x0 = jnp.concatenate(
            [block[p * fields_pad : (p + 1) * fields_pad] for p in range(pair)], axis=1
        )
        base[...] = x0
        lanes = base.shape[1]
        grow = jnp.concatenate(
            [jnp.full((1, 128), gl[b * pair + p], F32) for p in range(pair)], axis=1
        )
        first_pad = wt1.shape[0] // fields_pad
        low[0:fields_pad, :] = x0
        low[fields_pad:first_pad, :] = jnp.zeros((first_pad - fields_pad, lanes), F32)
        below = low[...]
        inputs = [below]
        total = jnp.zeros((1, lanes), F32)
        for k in range(3):
            maps_pad = wts[k].shape[0] // fields_pad
            below_b = below.astype(BF)
            for f in range(fields_pad):
                start = f * maps_pad
                if f < fields:
                    wide = jnp.broadcast_to(base[f : f + 1, :], (16, lanes)).astype(BF)
                    for t in range(maps_pad // 16):
                        outer[start + t * 16 : start + t * 16 + 16, :] = (
                            below_b[t * 16 : t * 16 + 16] * wide
                        )
                else:
                    outer[start : start + maps_pad, :] = jnp.zeros((maps_pad, lanes), BF)
            depth = fields_pad * maps_pad
            state = dot(wfs[k][...], outer[0:depth, :]).astype(BF).astype(F32)
            total = total + jnp.sum(state * owc[0:high, k : k + 1], axis=0, keepdims=True)
            states[k] = state
            below = state
        for p in range(pair):
            logit[b * pair + p] = jnp.sum(total[:, p * 128 : (p + 1) * 128])

        carried = jnp.zeros((high, lanes), F32)
        chunk = 8
        for k in (2, 1, 0):
            maps_pad = wts[k].shape[0] // fields_pad
            used = fields_pad if k == 0 else up(ow.shape[1], 8)
            grad_state = carried + owc[0:high, k : k + 1] * grow
            grad_low = jnp.concatenate(
                [grad_state.astype(BF), jnp.zeros((128 - high, lanes), BF)], axis=0
            )
            lower = low if k == 0 else states.at[k - 1]
            acc = jnp.zeros((used, lanes), F32)
            for c in range(0, fields, chunk):
                many = min(chunk, fields_pad - c)
                g = dot(wts[k][c * maps_pad : (c + many) * maps_pad, :], grad_low)
                for f in range(c, min(c + many, fields)):
                    gf = g[(f - c) * maps_pad : (f - c) * maps_pad + used]
                    acc = acc + gf * base[f : f + 1, :]
                    part = jnp.sum(gf * lower[0:used, :], axis=0, keepdims=True)
                    if k == 2:
                        ge[f : f + 1, :] = part
                    else:
                        ge[f : f + 1, :] += part
            if k > 0:
                carried = jnp.concatenate(
                    [acc, jnp.zeros((high - used, lanes), F32)], axis=0
                )
            else:
                carried = acc
        out = ge[...] + carried[0:fields_pad]
        keep = lax.broadcasted_iota(jnp.int32, out.shape, 0) < fields
        out = jnp.where(keep, out, 0.0).astype(BF)
        gmine[b] = jnp.concatenate(
            [out[:, p * 128 : (p + 1) * 128] for p in range(pair)], axis=0
        )
        for k in range(1, n_s):
            spread_copy(b, k).start()
        gall[me_s, b] = gmine[b]

    blocks = gmine.shape[0]
    for b in range(blocks):
        for k in range(1, n_s):
            spread_wait(b, k).wait_recv()
    mine = (me_s * part).astype(F32)
    first_slot = (me_s * cap_pad).astype(F32)
    hot_sum = jnp.zeros((part, 128), F32)
    for d in range(n_s):
        terms = jnp.concatenate([gall[d, b] for b in range(blocks)], axis=0)
        hot_r = asked[d, 1:2, 0:looks] - mine
        slot_r = asked[d, 2:3, 0:looks] - first_slot
        at = jnp.concatenate(
            [
                jnp.where(hot_r == iota((part, looks), 0), 1.0, 0.0),
                jnp.where(slot_r == iota((cap_pad, looks), 0), 1.0, 0.0),
            ],
            axis=0,
        )
        both = dot(at.astype(BF), terms)
        hot_sum = hot_sum + both[0:part]
        inc[d] = both[part : part + cap_pad].astype(BF)
    hot_mid[...] = hot_sum.astype(BF)
    for k in range(1, n_g):
        group_copy(k, *hot_g).start()
    for k in range(1, n_g):
        group_copy(k, *cold_g).start()
    hot_all[me_g] = hot_mid[...]
    allin[me_g] = inc[...]

    for k in range(1, n_g):
        group_wait(k, *hot_g).wait_recv()
    total = hot_all[0].astype(F32)
    for d in range(1, n_g):
        total = total + hot_all[d].astype(F32)
    hot_slice(me_s)[...] = total.astype(BF)
    for k in range(1, n_s):
        shard_copy(k, *hot_f).start()

    for k in range(1, n_g):
        group_wait(k, *id_g).wait_recv()
        group_wait(k, *cold_g).wait_recv()
    terms = jnp.concatenate(
        [allin[q, d] for q in range(n_g) for d in range(n_s)], axis=0
    )
    step = 512 if shard_rows % 512 == 0 else shard_rows

    @pl.loop(0, shard_rows // step)
    def _(t):
        first = pl.multiple_of(t * step, step)
        here = iota((step, slots), 0) + first.astype(F32)
        at = jnp.concatenate(
            [
                jnp.where(ids_all[q][0:1, 0:slots] == here, 1.0, 0.0).astype(BF)
                for q in range(n_g)
            ],
            axis=1,
        )
        cold_out[pl.ds(first, step), :] = dot(at, terms).astype(BF)

    for k in range(1, n_s):
        shard_wait(k, *hot_f).wait_recv()
    for k in range(1, n_s):
        for b in range(blocks):
            spread_copy(b, k).wait_send()
        shard_copy(k, *hot_f).wait_send()
    for k in range(1, n_g):
        group_copy(k, *id_g).wait_send()
        group_copy(k, *cold_g).wait_send()
        group_copy(k, *hot_g).wait_send()


def local(
    hot_row, cold_row, cold_owner, is_cold, grad_logit, hot_table, cold_table,
    first_weight, second_weight, third_weight, out_weight,
):
    n_g, n_s = lax.axis_size("group"), lax.axis_size("shard")
    samples, fields = hot_row.shape
    breadth = hot_table.shape[1]
    maps = out_weight.shape[1]
    cap_pad = up(samples * fields // n_s, 16)
    slots = n_s * cap_pad
    fields_pad = up(fields, 8)
    looks = samples * fields_pad
    first_pad, maps_pad = up(fields_pad, 16), up(maps, 16)
    depth1, depth2 = fields_pad * first_pad, fields_pad * maps_pad
    wide = up(max(slots, looks), 128)
    pair = 2
    lanes = pair * 128
    blocks = samples // pair
    part = hot_table.shape[0] // n_s
    vm = pl.BlockSpec(memory_space=pltpu.VMEM)
    sm = pl.BlockSpec(memory_space=pltpu.SMEM)
    hbm = pl.BlockSpec(memory_space=pl.ANY)
    sd = jax.ShapeDtypeStruct
    dma = pltpu.SemaphoreType.DMA
    V = pltpu.VMEM
    return pl.pallas_call(
        functools.partial(step_kernel, n_g, n_s),
        out_shape=(
            sd(hot_table.shape, BF), sd(cold_table.shape, BF), sd((samples,), F32)
        ),
        in_specs=[vm] * 4 + [sm] + [hbm] * 5 + [vm],
        out_specs=(vm, vm, sm),
        scratch_shapes=[
            V(hot_table.shape, BF), V(cold_table.shape, BF), V(first_weight.shape, BF),
            V(second_weight.shape, BF), V(third_weight.shape, BF),
            V((looks, breadth), BF),
            V((depth1, 128), BF), V((maps_pad, depth1), BF),
            V((depth2, 128), BF), V((maps_pad, depth2), BF),
            V((depth2, 128), BF), V((maps_pad, depth2), BF),
            V((128, 128), F32), V((8, wide), F32),
            V((128, 128), F32), V((128, up(second_weight.shape[1], 128)), F32),
            V((depth2, 128), F32),
            V((n_s, 8, wide), F32), V((n_s, 8, wide), F32),
            V((n_s, cap_pad, breadth), BF), V((n_s, cap_pad, breadth), BF),
            V((depth2, lanes), BF), V((fields_pad, lanes), F32), V((first_pad, lanes), F32),
            V((3, maps_pad, lanes), F32), V((fields_pad, lanes), F32),
            V((blocks, pair * fields_pad, breadth), BF),
            V((n_s, blocks, pair * fields_pad, breadth), BF),
            V((n_s, cap_pad, breadth), BF), V((n_g, n_s, cap_pad, breadth), BF),
            V((n_g, 8, wide), F32), V((part, breadth), BF), V((n_g, part, breadth), BF),
            dma((5,)), dma((n_s,)), dma((n_s,)), dma((n_s,)), dma((n_s,)),
            dma((blocks, n_s)), dma((blocks, n_s)),
            dma((n_g,)), dma((n_g,)), dma((n_g,)), dma((n_g,)), dma((n_g,)), dma((n_g,)),
            dma((n_s,)), dma((n_s,)),
        ],
        compiler_params=pltpu.CompilerParams(
            collective_id=0, has_side_effects=True, vmem_limit_bytes=VMEM_LIMIT
        ),
        name="step",
    )(
        hot_row, cold_row, cold_owner, is_cold, grad_logit, hot_table, cold_table,
        first_weight, second_weight, third_weight, out_weight,
    )


def solution(mesh):
    rows = P(("group", "shard"), None)
    return jax.shard_map(
        local,
        mesh=mesh,
        in_specs=(
            rows, rows, rows, rows, P(("group", "shard")), P(), P("shard", None),
            P(), P(), P(), P(),
        ),
        out_specs=(P(), P("shard", None), P(("group", "shard"))),
        check_vma=False,
    )
```

time: 72.7 us -> 60.4 us (0.83); the launches traced: 71.7 us -> 60.2 us
  Pallas kernels: 66.8 us -> 56.1 us
  local copies, waits for them, and re-layouts: 4.24 us -> 3.45 us
    pallas_call x3 -> x1, Pallas kernels: 66.8 us -> 56.1 us  [local(): pl.pallas_call(functools.partial(step_kernel, n_g, n_s), out_shape=(sd(ho...]
    slice x1 -> x0, local copies, waits for them, and re-layouts: 1.31 us -> none  [local(): return (hot_grad, cold_grad, logit[:, 0])]
    unnamed x4 -> x7, local copies, waits for them, and re-layouts: 2.93 us -> 3.45 us
where the time goes in v2:
time: 60.4 us; the launch traced here: 60.2 us
  Pallas kernels  56.1 us (93%)
  local copies, waits for them, and re-layouts  3.45 us (6%)
  between operations  0.65 us (1%)
    pallas_call x1, Pallas kernels, local(): pl.pallas_call(functools.partial(step_kernel, n_g, n_s), out_shape=(sd(ho...  56.1 us
    unnamed x7, local copies, waits for them, and re-layouts  3.45 us

profile of v2, /device:TPU:0, one launch (start us, length us, event | category | flops | bytes accessed | tf_op | source)
XLA Modules:
  0.0 60.2 jit_solution(14501277930876721816)
XLA Ops:
  0.6 56.1 %step.1 = (bf16[2048,128]{1,0:T(8,128)(2,1)}, bf16[4096,128]{1,0:T(8,128)(2,1)}, f32[8]{0:T(128)}) custom-call(s32[8,39]{1,0:T(8,128)} %hot_row.1, s32[8,39]{1,0:T(8,128)} %cold_row.1, s32[8,39]{1,0:T(8,128)} %cold_owner.1, s32[8,39]{1,0:T(8,128)} %is_cold.1, f32[8]{0:T(128)} %gl.1, bf16[2048,128]{1,0:T(8,128)(2,1)} %hot_table.1, ...), custom_call_target="tpu_custom_call" | custom-call | tf_op jit(solution)/shard_map/step/pallas_call | solution.py:437
  56.8 0.0 copy-start
  56.8 2.0 %copy.17 = bf16[2048,128]{1,0:T(8,128)(2,1)} copy(bf16[2048,128]{1,0:T(8,128)(2,1)} %get-tuple-element.6) | data formatting | bytes 1048576
  58.7 0.0 copy-done
  58.7 0.0 copy-start.1
  58.7 1.0 %copy.18 = bf16[4096,128]{1,0:T(8,128)(2,1)} copy(bf16[4096,128]{1,0:T(8,128)(2,1)S(1)} %copy-done) | data formatting | bytes 2097152
  59.7 0.0 copy-done.1
  59.7 0.5 copy.19
Async XLA Ops:
  56.8 2.0 %copy-start = (bf16[4096,128]{1,0:T(8,128)(2,1)S(1)}, bf16[4096,128]{1,0:T(8,128)(2,1)}, u32[]{:S(2)}) copy-start(bf16[4096,128]{1,0:T(8,128)(2,1)} %get-tuple-element.7) | copy-start | bytes 3145732
  58.7 1.0 %copy-start.1 = (f32[8]{0:T(128)S(1)}, f32[8]{0:T(128)}, u32[]{:S(2)}) copy-start(f32[8]{0:T(128)} %get-tuple-element.8) | copy-start | bytes 100

commit v3 on v2

--- a/solution.py
+++ b/solution.py
@@ -89,6 +89,8 @@
     looks = samples * fields_pad
     cap_pad = fetched.shape[1]
     slots = n_s * cap_pad
+    tight = inc.shape[0] // n_s
+    tight_slots = n_s * tight
     hot_rows, shard_rows = hot_out.shape[0], cold_out.shape[0]
     part = hot_rows // n_s
     pair = base.shape[1] // 128
@@ -240,7 +242,8 @@
         rep_copy(k).start()
     fetched[me_s] = reply[me_s]
 
-    meta[...] = jnp.broadcast_to(as_row(ids_c, width), meta.shape)
+    tight_c = jnp.concatenate([turned2[0:tight, d : d + 1] for d in range(n_s)], axis=0)
+    meta[...] = jnp.broadcast_to(as_row(tight_c, width), meta.shape)
     for k in range(1, n_g):
         group_copy(k, *id_g).start()
     ids_all[me_g] = meta[...]
@@ -345,6 +348,7 @@
     mine = (me_s * part).astype(F32)
     first_slot = (me_s * cap_pad).astype(F32)
     hot_sum = jnp.zeros((part, 128), F32)
+    kept = []
     for d in range(n_s):
         terms = jnp.concatenate([gall[d, b] for b in range(blocks)], axis=0)
         hot_r = asked[d, 1:2, 0:looks] - mine
@@ -352,14 +356,15 @@
         at = jnp.concatenate(
             [
                 jnp.where(hot_r == iota((part, looks), 0), 1.0, 0.0),
-                jnp.where(slot_r == iota((cap_pad, looks), 0), 1.0, 0.0),
+                jnp.where(slot_r == iota((tight, looks), 0), 1.0, 0.0),
             ],
             axis=0,
         )
         both = dot(at.astype(BF), terms)
         hot_sum = hot_sum + both[0:part]
-        inc[d] = both[part : part + cap_pad].astype(BF)
+        kept.append(both[part : part + tight])
     hot_mid[...] = hot_sum.astype(BF)
+    inc[...] = jnp.concatenate(kept, axis=0).astype(BF)
     for k in range(1, n_g):
         group_copy(k, *hot_g).start()
     for k in range(1, n_g):
@@ -380,17 +385,17 @@
         group_wait(k, *id_g).wait_recv()
         group_wait(k, *cold_g).wait_recv()
     terms = jnp.concatenate(
-        [allin[q, d] for q in range(n_g) for d in range(n_s)], axis=0
+        [allin[q] for q in range(n_g)], axis=0
     )
     step = 512 if shard_rows % 512 == 0 else shard_rows
 
     @pl.loop(0, shard_rows // step)
     def _(t):
         first = pl.multiple_of(t * step, step)
-        here = iota((step, slots), 0) + first.astype(F32)
+        here = iota((step, tight_slots), 0) + first.astype(F32)
         at = jnp.concatenate(
             [
-                jnp.where(ids_all[q][0:1, 0:slots] == here, 1.0, 0.0).astype(BF)
+                jnp.where(ids_all[q][0:1, 0:tight_slots] == here, 1.0, 0.0).astype(BF)
                 for q in range(n_g)
             ],
             axis=1,
@@ -418,6 +423,8 @@
     breadth = hot_table.shape[1]
     maps = out_weight.shape[1]
     cap_pad = up(samples * fields // n_s, 16)
+    tight = up(samples * fields // n_s, 8)
+    tight = tight if n_s * tight % 16 == 0 else cap_pad
     slots = n_s * cap_pad
     fields_pad = up(fields, 8)
     looks = samples * fields_pad
@@ -457,7 +464,7 @@
             V((3, maps_pad, lanes), F32), V((fields_pad, lanes), F32),
             V((blocks, pair * fields_pad, breadth), BF),
             V((n_s, blocks, pair * fields_pad, breadth), BF),
-            V((n_s, cap_pad, breadth), BF), V((n_g, n_s, cap_pad, breadth), BF),
+            V((n_s * tight, breadth), BF), V((n_g, n_s * tight, breadth), BF),
             V((n_g, 8, wide), F32), V((part, breadth), BF), V((n_g, part, breadth), BF),
             dma((5,)), dma((n_s,)), dma((n_s,)), dma((n_s,)), dma((n_s,)),
             dma((blocks, n_s)), dma((blocks, n_s)),

time: 60.4 us -> 59.4 us (0.983)
  Pallas kernels: 56.1 us -> 55.1 us
    pallas_call x1, Pallas kernels: 56.1 us -> 55.1 us  [local(): pl.pallas_call(functools.partial(step_kernel, n_g, n_s), out_shape=(sd(ho...]
where the time goes in v3:
time: 59.4 us; the launch traced here: 59.2 us
  Pallas kernels  55.1 us (93%)
  local copies, waits for them, and re-layouts  3.45 us (6%)
  between operations  0.65 us (1%)
    pallas_call x1, Pallas kernels, local(): pl.pallas_call(functools.partial(step_kernel, n_g, n_s), out_shape=(sd(ho...  55.1 us
    unnamed x7, local copies, waits for them, and re-layouts  3.45 us

profile of v3, /device:TPU:0, one launch (start us, length us, event | category | flops | bytes accessed | tf_op | source)
XLA Modules:
  0.0 59.2 jit_solution(16797929835572706529)
XLA Ops:
  0.6 55.1 %step.1 = (bf16[2048,128]{1,0:T(8,128)(2,1)}, bf16[4096,128]{1,0:T(8,128)(2,1)}, f32[8]{0:T(128)}) custom-call(s32[8,39]{1,0:T(8,128)} %hot_row.1, s32[8,39]{1,0:T(8,128)} %cold_row.1, s32[8,39]{1,0:T(8,128)} %cold_owner.1, s32[8,39]{1,0:T(8,128)} %is_cold.1, f32[8]{0:T(128)} %gl.1, bf16[2048,128]{1,0:T(8,128)(2,1)} %hot_table.1, ...), custom_call_target="tpu_custom_call" | custom-call | tf_op jit(solution)/shard_map/step/pallas_call | solution.py:444
  55.8 0.0 copy-start
  55.8 2.0 %copy.17 = bf16[2048,128]{1,0:T(8,128)(2,1)} copy(bf16[2048,128]{1,0:T(8,128)(2,1)} %get-tuple-element.6) | data formatting | bytes 1048576
  57.8 0.0 copy-done
  57.8 0.0 copy-start.1
  57.8 1.0 %copy.18 = bf16[4096,128]{1,0:T(8,128)(2,1)} copy(bf16[4096,128]{1,0:T(8,128)(2,1)S(1)} %copy-done) | data formatting | bytes 2097152
  58.7 0.0 copy-done.1
  58.7 0.5 copy.19
Async XLA Ops:
  55.8 2.0 %copy-start = (bf16[4096,128]{1,0:T(8,128)(2,1)S(1)}, bf16[4096,128]{1,0:T(8,128)(2,1)}, u32[]{:S(2)}) copy-start(bf16[4096,128]{1,0:T(8,128)(2,1)} %get-tuple-element.7) | copy-start | bytes 3145732
  57.8 1.0 %copy-start.1 = (f32[8]{0:T(128)S(1)}, f32[8]{0:T(128)}, u32[]{:S(2)}) copy-start(f32[8]{0:T(128)} %get-tuple-element.8) | copy-start | bytes 100
